TPU v7x, 32 devices: a whole 2x2x4 slice. The times are simulated.
32 devices in a mesh: blocks: 2 (over x), mode: 16 (over z, y, core).
Axes of the slice: x: 2, y: 2, z: 4, core: 2. Of those that a mesh axis runs over, the one named last changes fastest.
Arguments:
- right_side: float32 [2, 8, 1024, 1024], P(None, 'blocks', 'mode'), parts along dimension 1, may hold values from -6 to 6
- classes: int32 [8, 1024, 1024], P('blocks', 'mode'), parts along dimension 0, may hold values from 0 to 7
- noise_table: float32 [8], replicated, may hold values from 0.05 to 1
- kernel_first: bfloat16 [1024, 1024], replicated, may hold values from -1 to 3, as said below
- kernel_second: bfloat16 [1024, 1024], replicated, may hold values from -1 to 3, as said below
- basis_first: bfloat16 [1024, 1024], replicated, may hold values from -1 to 2, as said below
- basis_second: bfloat16 [1024, 1024], replicated, may hold values from -1 to 2, as said below
- eigen_first: float32 [1024], replicated, may hold values from 0.5 to 4
- eigen_second: float32 [1024], P('mode'), may hold values from 0.5 to 4
Outputs:
- solution_field: float32 [2, 8, 1024, 1024], P(None, 'blocks', 'mode'), parts along dimension 1
- residual: float32 [2, 8, 1024, 1024], P(None, 'blocks', 'mode'), parts along dimension 1
There are 2 independent parts, one for each index of `blocks`. A program takes and returns all parts, laid end to end along the dimension named above; an argument that names none is the same for every part. Nothing has to cross between parts.
Inputs may be any that keep to these rules, and one draw needn't show every extreme that they name: `kernel_first`: symmetric positive definite. `kernel_second`: symmetric positive definite. `basis_first`: nonsingular. `basis_second`: nonsingular.
All inputs are finite; a program needn't handle non-finite values.
Results may differ from a plain program's by a relative error of at most 0.0003.
Values sent between devices are 32-bit elements; how exact they have to be, the bound alone decides.
A program may use at most 128 MiB of HBM per device.

v0:
```python
import jax
import jax.numpy as jnp
from jax import lax
from jax.sharding import PartitionSpec as P

NCLASS = 8
ITERS = 2


def along_rows(matrix, field):
    return jnp.einsum("jk,sprk->sprj", matrix, field, precision=lax.Precision.HIGHEST)


def rows_to_send(matrix, field, groups):
    result = jnp.einsum("kj,sprk->jspr", matrix, field, precision=lax.Precision.HIGHEST)
    return result.reshape(groups, -1)


def received_to_columns(matrix, received, shape5):
    groups, cols, samples, planes, rows = shape5
    block = received.reshape(shape5)
    reshaped = matrix.reshape(groups, rows, matrix.shape[1])
    return jnp.einsum("mri,mcspr->cspi", reshaped, block, precision=lax.Precision.HIGHEST)


def along_columns(matrix, columns):
    return jnp.einsum("ik,cspk->cspi", matrix, columns, precision=lax.Precision.HIGHEST)


def columns_to_send(matrix, columns, groups, rows):
    reshaped = matrix.reshape(groups, rows, matrix.shape[1])
    result = jnp.einsum("mrk,cspk->mcspr", reshaped, columns, precision=lax.Precision.HIGHEST)
    return result.reshape(groups, -1)


def received_to_rows(matrix, received, shape5):
    groups, cols, samples, planes, rows = shape5
    block = received.reshape(shape5)
    reshaped = matrix.reshape(matrix.shape[0], groups, cols)
    return jnp.einsum("jmc,mcspr->sprj", reshaped, block, precision=lax.Precision.HIGHEST)


def body(
    right_side,
    classes,
    noise_table,
    kernel_first,
    kernel_second,
    basis_first,
    basis_second,
    eigen_first,
    eigen_second,
):
    groups = lax.axis_size("mode")
    samples, planes, rows, width_two = right_side.shape
    cols = eigen_second.shape[0]
    shape5 = (groups, cols, samples, planes, rows)
    kern_one = kernel_first.astype(jnp.float32)
    kern_two = kernel_second.astype(jnp.float32)
    base_one = basis_first.astype(jnp.float32)
    base_two = basis_second.astype(jnp.float32)
    noise = jnp.zeros(classes.shape, jnp.float32)
    for level in range(NCLASS):
        noise = noise + jnp.where(classes == level, noise_table[level], 0.0)
    noise = noise[None]
    mean_noise = jnp.mean(noise_table)
    col_weights = 1.0 / (eigen_second[:, None] * eigen_first[None, :] + mean_noise)
    col_weights = col_weights[:, None, None, :]

    def spectral(field):
        outgoing = rows_to_send(base_two, field, groups)
        incoming = lax.all_to_all(outgoing, "mode", split_axis=0, concat_axis=0, tiled=True)
        return received_to_columns(base_one, incoming, shape5) * col_weights

    def precond_apply(field):
        weighted = spectral(field)
        columns = along_columns(base_one, weighted)
        outgoing = columns_to_send(base_one, weighted, groups, rows)
        kernel_send = columns_to_send(kern_one, columns, groups, rows)
        back, kernel_back = (
            lax.all_to_all(outgoing, "mode", split_axis=0, concat_axis=0, tiled=True),
            lax.all_to_all(kernel_send, "mode", split_axis=0, concat_axis=0, tiled=True),
        )
        z_field = received_to_rows(base_two, back, shape5)
        image = (
            along_rows(kern_two, received_to_rows(base_two, kernel_back, shape5)) + noise * z_field
        )
        return (z_field, image)

    def residual_inner(residual, z_field):
        return lax.psum(jnp.sum(residual * z_field), "mode")

    solution_field = jnp.zeros_like(right_side)
    residual = right_side
    z_field, image = precond_apply(residual)
    direction, along = (z_field, image)
    gamma = residual_inner(residual, z_field)
    for step in range(ITERS):
        curvature = lax.psum(jnp.sum(direction * along), "mode")
        alpha = gamma / curvature
        solution_field = solution_field + alpha * direction
        residual = residual - alpha * along
        if step + 1 < ITERS:
            z_field, image = precond_apply(residual)
            gamma_new = residual_inner(residual, z_field)
            ratio = gamma_new / gamma
            direction = z_field + ratio * direction
            along = image + ratio * along
            gamma = gamma_new
    return (solution_field, residual)


def solution(mesh):
    in_specs = (
        P(None, "blocks", "mode", None),
        P("blocks", "mode", None),
        P(),
        P(),
        P(),
        P(),
        P(),
        P(),
        P("mode"),
    )
    out_specs = (P(None, "blocks", "mode", None), P(None, "blocks", "mode", None))
    return jax.shard_map(body, mesh=mesh, in_specs=in_specs, out_specs=out_specs, check_vma=False)
```

profile of v0, /device:TPU:29, one launch (start us, length us, event | category | flops | bytes accessed | tf_op | source)
XLA Modules:
  0.0 575.2 jit_solution(399112543989142584)
XLA Ops:
  0.6 7.1 %fusion.30 = f32[1024,2,4,64]{0,3,2,1:T(8,128)} fusion(f32[2,4,64,1024]{3,2,1,0:T(8,128)} %param.9, bf16[1024,1024]{1,0:T(8,128)(2,1)} %param.15), kind=kOutput, calls=%fused_computation.38 | convolution fusion | flops 6442450944 | bytes 6291456 | tf_op jit(solution)/shard_map/kj,sprk->jspr/dot_general | solution.py:15
  12.5 6.5 %all_to_all.48 = f32[16,1,32768]{2,1,0:T(1,128)} reshape(f32[1024,2,4,64]{3,2,1,0:T(4,128)} %copy.41) | data formatting | bytes 4194304 | tf_op jit(solution)/shard_map/all_to_all | solution.py:72
  19.0 6.9 %all-to-all-start = ((f32[16,1,32768]{2,1,0:T(1,128)}), f32[16,1,32768]{2,1,0:T(1,128)}, u32[]{:S(2)}, u32[]{:S(2)}) async-start(f32[16,1,32768]{2,1,0:T(1,128)} %all_to_all.48), calls=%async_computation | async-start | bytes 4194304 | tf_op jit(solution)/shard_map/all_to_all | solution.py:72
  27.4 45.0 %all-to-all-done = f32[16,1,32768]{2,1,0:T(1,128)} async-done(((f32[16,1,32768]{2,1,0:T(1,128)}), f32[16,1,32768]{2,1,0:T(1,128)}, u32[]{:S(2)}, u32[]{:S(2)}) %all-to-all-start) | async-done | bytes 2097184 | tf_op jit(solution)/shard_map/all_to_all | solution.py:72
  72.3 8.0 %reduce = f32[16,32768]{1,0:T(8,128)} reduce(f32[16,1,32768]{2,1,0:T(1,128)} %all-to-all-done, f32[]{:T(128)} %constant.23), dimensions={1}, to_apply=%all_to_all.37.reduce_sub_computation | reduce | bytes 4194308 | tf_op jit(solution)/shard_map/all_to_all | solution.py:72
  85.7 7.0 %fusion.10 = f32[64,2,4,1024,1]{3,0,4,2,1:T(8,128)S(1)} fusion(bf16[16,64,1024,1,1]{2,1,0,4,3:T(8,128)(2,1)S(1)} %bitcast.162, f32[16,64,2,4,64]{4,3,2,1,0:T(4,128)} %reshape.94), kind=kOutput, calls=%fused_computation.10 | convolution fusion | flops 6442450944 | bytes 6291456 | tf_op jit(solution)/shard_map/mri,mcspr->cspi/dot_general | solution.py:23
  94.0 6.7 %convolution_bitcast_fusion.3 = f32[16,64,2,4,64]{4,1,0,3,2:T(8,128)S(1)} fusion(bf16[16,64,1024,1,1]{2,1,0,4,3:T(8,128)(2,1)S(1)} %bitcast.163, f32[64,2,4,1024,1]{3,0,4,2,1:T(8,128)S(1)} %fusion.10, f32[64,1024]{1,0:T(8,128)S(1)} %add_divide_fusion), kind=kOutput, calls=%fused_computation.15 | convolution fusion | flops 6442975232 | bytes 6553600 | tf_op jit(solution)/shard_map/mrk,cspk->mcspr/dot_general | solution.py:32
  105.5 6.5 %all_to_all.49 = f32[16,1,32768]{2,1,0:T(1,128)} reshape(f32[16,64,2,4,64]{4,3,2,1,0:T(4,128)} %copy.44) | data formatting | bytes 4194304 | tf_op jit(solution)/shard_map/all_to_all | solution.py:81
  123.2 6.8 %convolution_bitcast_fusion.2 = f32[16,64,2,4,64]{4,1,0,3,2:T(8,128)S(1)} fusion(bf16[16,64,1024,1,1]{2,1,0,4,3:T(8,128)(2,1)S(1)} %bitcast.170, f32[64,2,4,1024]{3,0,2,1:T(8,128)S(1)} %fusion.23), kind=kOutput, calls=%fused_computation.14 | convolution fusion | flops 6442450944 | bytes 6291456 | tf_op jit(solution)/shard_map/mrk,cspk->mcspr/dot_general | solution.py:32
  134.9 6.5 %all_to_all.50 = f32[16,1,32768]{2,1,0:T(1,128)} reshape(f32[16,64,2,4,64]{4,3,2,1,0:T(4,128)} %copy.48) | data formatting | bytes 4194304 | tf_op jit(solution)/shard_map/all_to_all | solution.py:82
  141.4 23.0 %all-to-all-done.1 = f32[16,1,32768]{2,1,0:T(1,128)} async-done(((f32[16,1,32768]{2,1,0:T(1,128)}), f32[16,1,32768]{2,1,0:T(1,128)}, u32[]{:S(2)}, u32[]{:S(2)}) %all-to-all-start.1) | async-done | bytes 2097184 | tf_op jit(solution)/shard_map/all_to_all | solution.py:81
  174.9 6.9 %select_add_fusion = f32[4,64,1024]{2,1,0:T(8,128)S(1)} fusion(s32[4,64,1024]{2,1,0:T(8,128)} %param.10, f32[]{:T(128)} %bitcast.36, f32[]{:T(128)} %bitcast.35, f32[]{:T(128)} %bitcast.34, f32[]{:T(128)} %bitcast.33, f32[]{:T(128)} %bitcast.32, f32[]{:T(128)} %bitcast.31, f32[]{:T(128)} %bitcast.30, f32[]{:T(128)} %bitcast.29), kind=kLoop, calls=%fused_computation.55 | loop fusion | flops 6029312 | bytes 2097184 | tf_op jit(solution)/shard_map/add | solution.py:64
  181.8 8.0 %reduce.1 = f32[16,32768]{1,0:T(8,128)} reduce(f32[16,1,32768]{2,1,0:T(1,128)} %all-to-all-done.1, f32[]{:T(128)} %constant.23), dimensions={1}, to_apply=%all_to_all.39.reduce_sub_computation | reduce | bytes 4194308 | tf_op jit(solution)/shard_map/all_to_all | solution.py:81
  195.5 21.3 %all-to-all-done.2 = f32[16,1,32768]{2,1,0:T(1,128)} async-done(((f32[16,1,32768]{2,1,0:T(1,128)}), f32[16,1,32768]{2,1,0:T(1,128)}, u32[]{:S(2)}, u32[]{:S(2)}) %all-to-all-start.2) | async-done | bytes 2097184 | tf_op jit(solution)/shard_map/all_to_all | solution.py:82
  216.8 8.0 %reduce.2 = f32[16,32768]{1,0:T(8,128)} reduce(f32[16,1,32768]{2,1,0:T(1,128)} %all-to-all-done.2, f32[]{:T(128)} %constant.23), dimensions={1}, to_apply=%all_to_all.41.reduce_sub_computation | reduce | bytes 4194308 | tf_op jit(solution)/shard_map/all_to_all | solution.py:82
  230.2 6.7 %fusion.8 = f32[2,4,64,1024,1]{3,2,4,1,0:T(8,128)S(1)} fusion(bf16[1024,16,64,1,1]{0,2,1,4,3:T(8,128)(2,1)} %bitcast.166, f32[16,64,2,4,64]{4,3,2,1,0:T(4,128)} %reshape.96), kind=kOutput, calls=%fused_computation.8 | convolution fusion | flops 6442450944 | bytes 6291456 | tf_op jit(solution)/shard_map/jmc,mcspr->sprj/dot_general | solution.py:40
  246.4 29.6 %all-reduce = (f32[]{:T(128)}, f32[]{:T(128)}) all-reduce(f32[]{:T(128)} %get-tuple-element.3, f32[]{:T(128)} %get-tuple-element.2), channel_id=1, replica_groups=mesh['blocks'=2,'mode'=16] {'mode'}, use_global_device_ids=true, to_apply=%region_2.3 | all-reduce | flops 2 | bytes 16 | tf_op jit(solution)/shard_map/psum | solution.py:91
  297.5 55.9 %all_to_all.60 = f32[16,1,32768]{2,1,0:T(1,128)} all-to-all(f32[16,1,32768]{2,1,0:T(1,128)} %all_to_all.51), channel_id=1, replica_groups=mesh['blocks'=2,'mode'=16] {'mode'}, dimensions={0} | all-to-all | bytes 4194304 | tf_op jit(solution)/shard_map/all_to_all | solution.py:72
  353.4 8.0 %reduce.3 = f32[16,32768]{1,0:T(8,128)} reduce(f32[16,1,32768]{2,1,0:T(1,128)} %all_to_all.60, f32[]{:T(128)} %constant.23), dimensions={1}, to_apply=%all_to_all.43.reduce_sub_computation | reduce | bytes 4194308 | tf_op jit(solution)/shard_map/all_to_all | solution.py:72
  366.8 6.8 %fusion.4 = f32[64,2,4,1024,1]{3,0,4,2,1:T(8,128)S(1)} fusion(bf16[16,64,1024,1,1]{2,1,0,4,3:T(8,128)(2,1)S(1)} %bitcast.164, f32[16,64,2,4,64]{4,3,2,1,0:T(4,128)} %reshape.100), kind=kOutput, calls=%fused_computation.4 | convolution fusion | flops 6442450944 | bytes 6291456 | tf_op jit(solution)/shard_map/mri,mcspr->cspi/dot_general | solution.py:23
  375.0 6.7 %convolution_bitcast_fusion.1 = f32[16,64,2,4,64]{4,1,0,3,2:T(8,128)S(1)} fusion(bf16[16,64,1024,1,1]{2,1,0,4,3:T(8,128)(2,1)S(1)} %bitcast.165, f32[64,2,4,1024,1]{3,0,4,2,1:T(8,128)S(1)} %fusion.4, f32[64,1024]{1,0:T(8,128)S(1)} %add_divide_fusion), kind=kOutput, calls=%fused_computation.13 | convolution fusion | flops 6442975232 | bytes 6553600 | tf_op jit(solution)/shard_map/mrk,cspk->mcspr/dot_general | solution.py:32
  386.4 6.5 %all_to_all.52 = f32[16,1,32768]{2,1,0:T(1,128)} reshape(f32[16,64,2,4,64]{4,3,2,1,0:T(4,128)} %copy.54) | data formatting | bytes 4194304 | tf_op jit(solution)/shard_map/all_to_all | solution.py:81
  404.2 6.8 %convolution_bitcast_fusion = f32[16,64,2,4,64]{4,1,0,3,2:T(8,128)S(1)} fusion(bf16[16,64,1024,1,1]{2,1,0,4,3:T(8,128)(2,1)S(1)} %bitcast.171, f32[64,2,4,1024]{3,0,2,1:T(8,128)S(1)} %fusion.21), kind=kOutput, calls=%fused_computation.12 | convolution fusion | flops 6442450944 | bytes 6291456 | tf_op jit(solution)/shard_map/mrk,cspk->mcspr/dot_general | solution.py:32
  415.9 6.5 %all_to_all.53 = f32[16,1,32768]{2,1,0:T(1,128)} reshape(f32[16,64,2,4,64]{4,3,2,1,0:T(4,128)} %copy.57) | data formatting | bytes 4194304 | tf_op jit(solution)/shard_map/all_to_all | solution.py:82
  422.4 23.0 %all-to-all-done.4 = f32[16,1,32768]{2,1,0:T(1,128)} async-done(((f32[16,1,32768]{2,1,0:T(1,128)}), f32[16,1,32768]{2,1,0:T(1,128)}, u32[]{:S(2)}, u32[]{:S(2)}) %all-to-all-start.4) | async-done | bytes 2097184 | tf_op jit(solution)/shard_map/all_to_all | solution.py:81
  451.2 8.0 %reduce.4 = f32[16,32768]{1,0:T(8,128)} reduce(f32[16,1,32768]{2,1,0:T(1,128)} %all-to-all-done.4, f32[]{:T(128)} %constant.23), dimensions={1}, to_apply=%all_to_all.45.reduce_sub_computation | reduce | bytes 4194308 | tf_op jit(solution)/shard_map/all_to_all | solution.py:81
  464.6 9.3 %fusion.25 = (f32[]{:T(128)}, f32[2,4,64,1024,1]{3,2,4,1,0:T(8,128)}) fusion(f32[2,4,64,1024]{3,2,1,0:T(8,128)} %copy-done.4, bf16[1024,16,64,1,1]{0,2,1,4,3:T(8,128)(2,1)} %bitcast.167, f32[16,64,2,4,64]{4,3,2,1,0:T(4,128)} %reshape.101), kind=kOutput, calls=%fused_computation.32 | convolution fusion | flops 6443499520 | bytes 8388612 | tf_op jit(solution)/shard_map/jmc,mcspr->sprj/dot_general | solution.py:40
  473.9 35.4 %psum.30 = f32[]{:T(128)} all-reduce(f32[]{:T(128)} %get-tuple-element.15), channel_id=1, replica_groups=mesh['blocks'=2,'mode'=16] {'mode'}, use_global_device_ids=true, to_apply=%region_6.7 | all-reduce | flops 1 | bytes 8 | tf_op jit(solution)/shard_map/psum | solution.py:91
  510.6 7.9 %reduce.5 = f32[16,32768]{1,0:T(8,128)} reduce(f32[16,1,32768]{2,1,0:T(1,128)} %all-to-all-done.5, f32[]{:T(128)} %constant.23), dimensions={1}, to_apply=%all_to_all.47.reduce_sub_computation | reduce | bytes 4194308 | tf_op jit(solution)/shard_map/all_to_all | solution.py:82
  523.9 6.7 %fusion = f32[2,4,64,1024,1]{3,2,4,1,0:T(8,128)S(1)} fusion(bf16[1024,16,64,1,1]{0,2,1,4,3:T(8,128)(2,1)} %bitcast.168, f32[16,64,2,4,64]{4,3,2,1,0:T(4,128)} %reshape.102), kind=kOutput, calls=%fused_computation | convolution fusion | flops 6442450944 | bytes 6291456 | tf_op jit(solution)/shard_map/jmc,mcspr->sprj/dot_general | solution.py:40
  536.6 30.2 %psum.31 = f32[]{:T(128)} all-reduce(f32[]{:T(128)} %get-tuple-element.17), channel_id=1, replica_groups=mesh['blocks'=2,'mode'=16] {'mode'}, use_global_device_ids=true, to_apply=%region_8.9 | all-reduce | flops 1 | bytes 8 | tf_op jit(solution)/shard_map/psum | solution.py:99
  568.1 7.0 %fusion.36 = (f32[2,4,64,1024]{3,2,1,0:T(8,128)}, f32[2,4,64,1024]{3,2,1,0:T(8,128)}) fusion(f32[2,4,64,1024,1]{3,2,4,1,0:T(8,128)} %copy-done.2, f32[]{:T(128)S(6)} %div.27, f32[]{:T(128)S(6)} %div.26, f32[2,4,64,1024,1]{3,2,4,1,0:T(8,128)} %get-tuple-element.16, f32[]{:T(128)S(6)} %div.25, f32[2,4,64,1024]{3,2,1,0:T(8,128)} %copy-done.4, ...), kind=kLoop, calls=%fused_computation.49 | loop fusion | flops 3670016 | bytes 12582924 | tf_op jit(solution)/shard_map/add | solution.py:101
  (67 shorter events, 134.5 us)
Async XLA Ops:
  0.6 85.1 %copy-start = (bf16[1024,1024]{1,0:T(8,128)(2,1)S(1)}, bf16[1024,1024]{1,0:T(8,128)(2,1)}, u32[]{:S(2)}) copy-start(bf16[1024,1024]{1,0:T(8,128)(2,1)} %param.14) | copy-start | bytes 6291460
  19.0 6.9 %copy-start.12 = (f32[8]{0:T(128)S(1)}, f32[8]{0:T(128)}, u32[]{:S(2)}) copy-start(f32[8]{0:T(128)} %param.11) | copy-start | bytes 100
  19.0 8.2 %copy-start.13 = (f32[1024]{0:T(1024)S(1)}, f32[1024]{0:T(1024)}, u32[]{:S(2)}) copy-start(f32[1024]{0:T(1024)} %param.16) | copy-start | bytes 12292
  19.0 8.2 %copy-start.14 = (f32[64]{0:T(128)S(1)}, f32[64]{0:T(128)}, u32[]{:S(2)}) copy-start(f32[64]{0:T(128)} %param.17) | copy-start | bytes 772
  19.0 53.3 %all-to-all-start = ((f32[16,1,32768]{2,1,0:T(1,128)}), f32[16,1,32768]{2,1,0:T(1,128)}, u32[]{:S(2)}, u32[]{:S(2)}) async-start(f32[16,1,32768]{2,1,0:T(1,128)} %all_to_all.48), calls=%async_computation | async-start | bytes 4194304 | tf_op jit(solution)/shard_map/all_to_all | solution.py:72
  92.7 1.3 copy-start.18
  111.9 52.4 %all-to-all-start.1 = ((f32[16,1,32768]{2,1,0:T(1,128)}), f32[16,1,32768]{2,1,0:T(1,128)}, u32[]{:S(2)}, u32[]{:S(2)}) async-start(f32[16,1,32768]{2,1,0:T(1,128)} %all_to_all.49), calls=%async_computation.1 | async-start | bytes 4194304 | tf_op jit(solution)/shard_map/all_to_all | solution.py:81
  118.0 5.2 copy-start.15
  164.4 52.4 %all-to-all-start.2 = ((f32[16,1,32768]{2,1,0:T(1,128)}), f32[16,1,32768]{2,1,0:T(1,128)}, u32[]{:S(2)}, u32[]{:S(2)}) async-start(f32[16,1,32768]{2,1,0:T(1,128)} %all_to_all.50), calls=%async_computation.2 | async-start | bytes 4194304 | tf_op jit(solution)/shard_map/all_to_all | solution.py:82
  230.2 6.7 %copy-start.1 = (bf16[1024,1024]{0,1:T(8,128)(2,1)S(1)}, bf16[1024,1024]{0,1:T(8,128)(2,1)}, u32[]{:S(2)}) copy-start(bf16[1024,1024]{0,1:T(8,128)(2,1)} %copy.46) | copy-start | bytes 6291460
  230.2 6.7 %copy-start.7 = (f32[16,64,2,4,64]{4,3,2,1,0:T(4,128)S(1)}, f32[16,64,2,4,64]{4,3,2,1,0:T(4,128)}, u32[]{:S(2)}) copy-start(f32[16,64,2,4,64]{4,3,2,1,0:T(4,128)} %reshape.99) | copy-start | bytes 6291460
  236.9 3.9 copy-start.2
  236.9 3.9 copy-start.8
  236.9 3.9 copy-start.9
  277.3 4.2 copy-start.11
  280.1 1.3 copy-start.4
  373.7 1.3 copy-start.17
  392.9 52.4 %all-to-all-start.4 = ((f32[16,1,32768]{2,1,0:T(1,128)}), f32[16,1,32768]{2,1,0:T(1,128)}, u32[]{:S(2)}, u32[]{:S(2)}) async-start(f32[16,1,32768]{2,1,0:T(1,128)} %all_to_all.52), calls=%async_computation.4 | async-start | bytes 4194304 | tf_op jit(solution)/shard_map/all_to_all | solution.py:81
  399.0 5.2 copy-start.16
  445.4 65.2 %all-to-all-start.5 = ((f32[16,1,32768]{2,1,0:T(1,128)}), f32[16,1,32768]{2,1,0:T(1,128)}, u32[]{:S(2)}, u32[]{:S(2)}) async-start(f32[16,1,32768]{2,1,0:T(1,128)} %all_to_all.53), calls=%async_computation.5 | async-start | bytes 4194304 | tf_op jit(solution)/shard_map/all_to_all | solution.py:82
  523.9 6.7 %copy-start.3 = (f32[2,4,64,1024,1]{3,2,4,1,0:T(8,128)S(1)}, f32[2,4,64,1024,1]{3,2,4,1,0:T(8,128)}, u32[]{:S(2)}) copy-start(f32[2,4,64,1024,1]{3,2,4,1,0:T(8,128)} %copy-done.2) | copy-start | bytes 6291460
  523.9 6.7 %copy-start.5 = (f32[2,4,64,1024]{3,2,1,0:T(8,128)S(1)}, f32[2,4,64,1024]{3,2,1,0:T(8,128)}, u32[]{:S(2)}) copy-start(f32[2,4,64,1024]{3,2,1,0:T(8,128)} %get-tuple-element.14) | copy-start | bytes 6291460
  523.9 6.7 %copy-start.6 = (f32[2,4,64,1024,1]{3,2,4,1,0:T(8,128)S(1)}, f32[2,4,64,1024,1]{3,2,4,1,0:T(8,128)}, u32[]{:S(2)}) copy-start(f32[2,4,64,1024,1]{3,2,4,1,0:T(8,128)} %get-tuple-element.16) | copy-start | bytes 6291460
  523.9 6.7 %copy-start.10 = (bf16[1024,1024]{1,0:T(8,128)(2,1)S(1)}, bf16[1024,1024]{1,0:T(8,128)(2,1)}, u32[]{:S(2)}) copy-start(bf16[1024,1024]{1,0:T(8,128)(2,1)} %param.13) | copy-start | bytes 6291460
where the time goes:
time: 587 us; the launch traced here: 575 us
  blocking collectives  151 us (26%)
  waiting for transfers between devices  112 us (19%)
  local copies, waits for them, and re-layouts  109 us (19%)
  matrix products  101 us (17%)
  other arithmetic  65.3 us (11%)
  starting transfers between devices  30.7 us (5%)
    psum x2, blocking collectives, residual_inner(): return lax.psum(jnp.sum(residual * z_field), 'mode')  65 us
    all_to_all x1, blocking collectives, spectral(): lax.all_to_all(outgoing, 'mode', split_axis=0, concat_axis=0, tiled=True)  55.9 us
    all_to_all x2, waiting for transfers between devices, precond_apply(): lax.all_to_all(outgoing, 'mode', split_axis=0, concat_axis=0, tiled=True)  45.9 us
    all_to_all x1, waiting for transfers between devices, spectral(): lax.all_to_all(outgoing, 'mode', split_axis=0, concat_axis=0, tiled=True)  45 us
    psum x1, blocking collectives, body(): curvature = lax.psum(jnp.sum(direction * along), 'mode')  30.2 us
    dot_general x4, matrix products, columns_to_send(): jnp.einsum('mrk,cspk->mcspr', reshaped, columns, precision=lax.Precision....  27 us
    dot_general x4, matrix products, received_to_rows(): jnp.einsum('jmc,mcspr->sprj', reshaped, block, precision=lax.Precision.HI...  26.5 us
    reshape x4, local copies, waits for them, and re-layouts, received_to_rows(): block = received.reshape(shape5)  21.9 us
  transfers between devices with their start and end apart: 5, of which 4 were waited for; matrix products, arithmetic and copies ran while one was open for 14% of the time, Pallas kernels for 0%

commit v1 on v0

v1 whole, which is shorter than its diff:
```python
import jax
import jax.numpy as jnp
from jax import lax
from jax.sharding import PartitionSpec as P

ITERS = 2


def split(field):
    high = lax.reduce_precision(field, 8, 7)
    return high.astype(jnp.bfloat16), (field - high).astype(jnp.bfloat16)


def dot(left, right, dims):
    return lax.dot_general(left, right, (dims, ((), ())), preferred_element_type=jnp.float32)


def on_first(matrix, field, transposed=False):
    dims = ((0 if transposed else 1,), (0,))
    high, low = split(field)
    return dot(matrix, high, dims) + dot(matrix, low, dims)


def on_second(matrix, field, transposed=False):
    dims = ((1,), (0 if transposed else 1,))
    high, low = split(field)
    return dot(high, matrix, dims) + dot(low, matrix, dims)


def body(
    right_side,
    classes,
    noise_table,
    kernel_first,
    kernel_second,
    basis_first,
    basis_second,
    eigen_first,
    eigen_second,
):
    devices = lax.axis_size("mode")
    samples, planes, rows, width = right_side.shape
    height = eigen_first.shape[0]
    fields = samples * planes
    share = devices // fields
    cols = width // share
    near = [[f * share + c for c in range(share)] for f in range(fields)]
    twins = [
        [(p * samples + s) * share + c for s in range(samples)]
        for p in range(planes)
        for c in range(share)
    ]
    me = lax.axis_index("mode")
    mine = lax.rem(me, share)

    def to_all(blocks):
        return lax.all_to_all(blocks, "mode", split_axis=0, concat_axis=0, tiled=True)

    def to_rows(field):
        return lax.all_to_all(
            field, "mode", split_axis=0, concat_axis=1, axis_index_groups=near, tiled=True
        )

    def to_columns(field):
        return lax.all_to_all(
            field, "mode", split_axis=1, concat_axis=0, axis_index_groups=near, tiled=True
        )

    def give_back(field):
        got = to_all(field.reshape(devices, rows, cols))
        got = got.reshape(planes, samples, share, rows, cols)
        return got.transpose(1, 0, 3, 2, 4).reshape(right_side.shape)

    level = jnp.take(noise_table, 0) * jnp.ones(classes.shape, jnp.float32)
    for index in range(1, noise_table.shape[0]):
        level = jnp.where(classes == index, noise_table[index], level)
    mean_noise = jnp.mean(noise_table)

    part = cols // samples
    outgoing = level.reshape(planes, rows, share, samples, part).transpose(0, 3, 2, 1, 4)
    quarter = to_all(outgoing.reshape(devices, rows, part)).reshape(height, part)
    noise = lax.all_gather(quarter, "mode", axis=1, axis_index_groups=twins, tiled=True)

    all_second = lax.all_gather(eigen_second, "mode", tiled=True)
    weights = 1.0 / (eigen_first[:, None] * all_second[None, :] + mean_noise)
    row_count = height // share
    row_weights = lax.dynamic_slice_in_dim(weights, mine * row_count, row_count, 0)
    col_weights = lax.dynamic_slice_in_dim(weights, mine * cols, cols, 1)

    turned = on_second(basis_second, right_side.reshape(-1, width), True)
    outgoing = turned.reshape(samples, planes, rows, share, cols).transpose(1, 0, 3, 2, 4)
    incoming = to_all(outgoing.reshape(devices, rows, cols)).reshape(height, cols)

    spectrum = on_first(basis_first, incoming, True)
    weighted = col_weights * spectrum
    gamma_part = jnp.sum(spectrum * weighted)
    spectrum_rows = to_rows(spectrum)
    direction_rows = on_second(basis_second, to_rows(on_first(basis_first, weighted)))
    direction = to_columns(direction_rows)
    image = on_first(kernel_first, to_columns(on_second(kernel_second, direction_rows)))
    image = image + noise * direction
    curve_part = jnp.sum(direction * image)
    gamma, curvature = lax.psum(jnp.stack([gamma_part, curve_part]), "mode")
    alpha = gamma / curvature
    change = on_second(basis_second, to_rows(on_first(basis_first, image, True)), True)
    spectrum_rows = spectrum_rows - alpha * change
    weighted = row_weights * spectrum_rows
    gamma_part = jnp.sum(spectrum_rows * weighted)
    later_rows = to_columns(on_second(basis_second, weighted))
    later = on_first(basis_first, later_rows)
    later_image = on_first(kernel_first, to_columns(on_second(kernel_second, to_rows(later))))
    later_image = later_image + noise * later
    parts = jnp.stack([gamma_part, jnp.sum(later * later_image), jnp.sum(later * image)])
    gamma_new, own, cross = lax.psum(parts, "mode")
    ratio = gamma_new / gamma
    step = gamma_new / (own + ratio * (2.0 * cross + ratio * curvature))
    before = alpha + step * ratio
    solution_field = give_back(before * direction + step * later)
    applied = give_back(before * image + step * later_image)
    return solution_field, right_side - applied


def solution(mesh):
    in_specs = (
        P(None, "blocks", "mode", None),
        P("blocks", "mode", None),
        P(),
        P(),
        P(),
        P(),
        P(),
        P(),
        P("mode"),
    )
    out_specs = (P(None, "blocks", "mode", None), P(None, "blocks", "mode", None))
    return jax.shard_map(body, mesh=mesh, in_specs=in_specs, out_specs=out_specs, check_vma=False)
```

time: 587 us -> 447 us (0.76)
  local copies, waits for them, and re-layouts: 109 us -> 53.4 us
  matrix products: 101 us -> 52.8 us
  other arithmetic: 65.3 us -> 32 us
  waiting for transfers between devices: 112 us -> 92.5 us
  between operations: 5.65 us -> 21.2 us
    unnamed x0 -> x1, blocking collectives: none -> 55.2 us
    dot_general x16 -> x24, matrix products: 101 us -> 52.8 us  [dot(): lax.dot_general(left, right, (dims, ((), ())), preferred_element_type=jnp...]
    all_to_all x6 -> x0, other arithmetic: 47.8 us -> none  [the longest x2 16 us: spectral(): lax.all_to_all(outgoing, 'mode', split_axis=0, concat_axis=0, tiled=True)]
    psum x3 -> x2, blocking collectives: 95.2 us -> 58.9 us  [the longest x1 29.9 us: body(): gamma_new, own, cross = lax.psum(parts, 'mode')]
    all_to_all x6 -> x9, local copies, waits for them, and re-layouts: 39 us -> 5.77 us  [the longest x5 3.64 us: to_columns(): lax.all_to_all(field, 'mode', split_axis=1, concat_axis=0, axis_index_gro...]
    all_to_all x5, waiting for transfers between devices: 112 us -> 92.4 us  [the longest x4 92.4 us: to_all(): lax.all_to_all(blocks, 'mode', split_axis=0, concat_axis=0, tiled=True)]
    all_to_all x1 -> x7, blocking collectives: 55.9 us -> 40.7 us  [the longest x4 22.6 us: to_columns(): lax.all_to_all(field, 'mode', split_axis=1, concat_axis=0, axis_index_gro...]
    reshape x6 -> x7, local copies, waits for them, and re-layouts: 32.7 us -> 20.9 us  [the longest x2 8.01 us: give_back(): return got.transpose(1, 0, 3, 2, 4).reshape(right_side.shape)]
  transfers between devices with their start and end apart: 5 -> 6, of which waited for: 4 -> 3; matrix products, arithmetic and copies ran while one was open for 14% -> 13% of each run, Pallas kernels for 0% -> 0%
where the time goes in v1:
time: 447 us; the launch traced here: 440 us
  blocking collectives  155 us (35%)
  waiting for transfers between devices  92.5 us (21%)
  local copies, waits for them, and re-layouts  53.4 us (12%)
  matrix products  52.8 us (12%)
  starting transfers between devices  33 us (7%)
  other arithmetic  32 us (7%)
  between operations  21.2 us (5%)
    all_to_all x4, waiting for transfers between devices, to_all(): lax.all_to_all(blocks, 'mode', split_axis=0, concat_axis=0, tiled=True)  92.4 us
    unnamed x1, blocking collectives  55.2 us
    dot_general x24, matrix products, dot(): lax.dot_general(left, right, (dims, ((), ())), preferred_element_type=jnp...  52.8 us
    psum x1, blocking collectives, body(): gamma_new, own, cross = lax.psum(parts, 'mode')  29.9 us
    psum x1, blocking collectives, body(): gamma, curvature = lax.psum(jnp.stack([gamma_part, curve_part]), 'mode')  28.9 us
    all_to_all x4, starting transfers between devices, to_all(): lax.all_to_all(blocks, 'mode', split_axis=0, concat_axis=0, tiled=True)  27.7 us
    all_to_all x4, blocking collectives, to_columns(): lax.all_to_all(field, 'mode', split_axis=1, concat_axis=0, axis_index_gro...  22.6 us
    all_to_all x3, blocking collectives, to_rows(): lax.all_to_all(field, 'mode', split_axis=0, concat_axis=1, axis_index_gro...  18.1 us
  transfers between devices with their start and end apart: 6, of which 3 were waited for; matrix products, arithmetic and copies ran while one was open for 13% of the time, Pallas kernels for 0%

profile of v1, /device:TPU:29, one launch (start us, length us, event | category | flops | bytes accessed | tf_op | source)
XLA Modules:
  0.0 439.5 jit_solution(13590148112618049821)
XLA Ops:
  8.8 6.9 %select_select_fusion = f32[4,64,1024]{2,1,0:T(8,128)S(1)} fusion(s32[4,64,1024]{2,1,0:T(8,128)} %param.10, f32[]{:T(128)} %bitcast.24, f32[]{:T(128)} %bitcast.23, f32[]{:T(128)} %bitcast.22, f32[]{:T(128)} %bitcast.21, f32[]{:T(128)} %bitcast.20, f32[]{:T(128)} %bitcast.19, f32[]{:T(128)} %bitcast.18, f32[]{:T(128)} %bitcast.17), kind=kLoop, calls=%fused_computation.75 | loop fusion | flops 3670016 | bytes 2097184 | tf_op jit(solution)/shard_map/jit(_where)/select_n | solution.py:76
  19.9 6.3 %all-to-all-start.4 = ((f32[16,64,256]{2,1,0:T(8,128)}), f32[16,64,256]{2,1,0:T(8,128)S(1)}, u32[]{:S(2)}, u32[]{:S(2)}) async-start(f32[16,64,256]{2,1,0:T(8,128)} %bitcast.198), calls=%async_computation.4 | async-start | bytes 2097152 | tf_op jit(solution)/shard_map/all_to_all | solution.py:57
  32.2 4.0 reshape.73
  36.1 3.3 copy.35
  39.4 10.8 %all-to-all-done.4 = f32[16,64,256]{2,1,0:T(8,128)S(1)} async-done(((f32[16,64,256]{2,1,0:T(8,128)}), f32[16,64,256]{2,1,0:T(8,128)S(1)}, u32[]{:S(2)}, u32[]{:S(2)}) %all-to-all-start.4) | async-done | bytes 1048608 | tf_op jit(solution)/shard_map/all_to_all | solution.py:57
  50.2 6.0 %all-to-all-start = ((f32[16,64,512]{2,1,0:T(8,128)}), f32[16,64,512]{2,1,0:T(8,128)}, u32[]{:S(2)}, u32[]{:S(2)}) async-start(f32[16,64,512]{2,1,0:T(8,128)} %bitcast.184), calls=%async_computation | async-start | bytes 4194304 | tf_op jit(solution)/shard_map/all_to_all | solution.py:57
  59.1 55.2 %all-reduce = f32[1024]{0:T(1024)S(1)} all-reduce(f32[1024]{0:T(1024)S(1)} %dynamic-update-slice.1), channel_id=1, replica_groups=mesh['blocks'=2,'mode'=16] {'mode'}, use_global_device_ids=true, to_apply=%add | all-reduce | flops 1024 | bytes 8192
  127.7 6.7 %all_to_all.172 = f32[2,512,512]{1,2,0:T(8,128)S(1)} all-to-all(f32[2,512,512]{1,2,0:T(8,128)S(1)} %bitcast.188), channel_id=1, replica_groups={{0,1},{2,3},{4,5},{6,7},{8,9},{10,11},{12,13},{14,15},{16,17},{18,19},{..., dimensions={0} | all-to-all | bytes 4194304 | tf_op jit(solution)/shard_map/all_to_all | solution.py:60
  138.7 6.4 %all_to_all.173 = f32[512,2,512]{2,0,1:T(8,128)} all-to-all(f32[512,2,512]{2,0,1:T(8,128)S(1)} %bitcast.194), channel_id=1, replica_groups={{0,1},{2,3},{4,5},{6,7},{8,9},{10,11},{12,13},{14,15},{16,17},{18,19},{..., dimensions={1} | all-to-all | bytes 4194304 | tf_op jit(solution)/shard_map/all_to_all | solution.py:65
  148.0 3.7 fusion.21
  153.2 5.6 %all_to_all.174 = f32[512,2,512]{2,0,1:T(8,128)S(1)} all-to-all(f32[512,2,512]{2,0,1:T(8,128)S(1)} %bitcast.190), channel_id=1, replica_groups={{0,1},{2,3},{4,5},{6,7},{8,9},{10,11},{12,13},{14,15},{16,17},{18,19},{..., dimensions={1} | all-to-all | bytes 4194304 | tf_op jit(solution)/shard_map/all_to_all | solution.py:65
  162.9 7.0 %multiply_reduce_fusion.1 = (f32[]{:T(128)}, f32[1024,512]{0,1:T(8,128)}) fusion(f32[1024,512]{0,1:T(8,128)} %copy.55, f32[1024,512]{0,1:T(8,128)} %all-gather.2.cloned.1.call-done, f32[512,1024]{1,0:T(8,128)} %fusion.34, bf16[1024,512]{1,0:T(8,128)(2,1)S(1)} %get-tuple-element.23, bf16[1024,1024]{1,0:T(8,128)(2,1)} %param.12), kind=kOutput, calls=%fused_computation.61 | convolution fusion | flops 1076363264 | bytes 11534340 | tf_op jit(solution)/shard_map/dot_general | solution.py:15
  172.8 28.9 %psum.14 = f32[2]{0:T(128)S(1)} all-reduce(f32[2]{0:T(128)S(1)} %pad_maximum_fusion), channel_id=1, replica_groups=mesh['blocks'=2,'mode'=16] {'mode'}, use_global_device_ids=true, to_apply=%region_3.4 | all-reduce | flops 2 | bytes 16 | tf_op jit(solution)/shard_map/psum | solution.py:103
  202.3 3.6 fusion.22
  207.4 6.0 %all_to_all.175 = f32[2,512,512]{1,2,0:T(8,128)} all-to-all(f32[2,512,512]{1,2,0:T(8,128)S(1)} %bitcast.191), channel_id=1, replica_groups={{0,1},{2,3},{4,5},{6,7},{8,9},{10,11},{12,13},{14,15},{16,17},{18,19},{..., dimensions={0} | all-to-all | bytes 4194304 | tf_op jit(solution)/shard_map/all_to_all | solution.py:60
  213.4 5.2 %all-to-all-start.5 = ((f32[2,512,512]{1,2,0:T(8,128)}), f32[2,512,512]{1,2,0:T(8,128)}, u32[]{:S(2)}, u32[]{:S(2)}) async-start(f32[2,512,512]{1,2,0:T(8,128)} %bitcast.185), calls=%async_computation.5 | async-start | bytes 4194304 | tf_op jit(solution)/shard_map/all_to_all | solution.py:60
  224.4 5.3 %multiply_reduce_fusion = (f32[]{:T(128)}, f32[512,1024]{0,1:T(8,128)S(1)}) fusion(f32[1024,1024]{0,1:T(8,128)} %add_divide_fusion, s32[]{:T(128)S(6)} %select_n.31, f32[512,1024]{0,1:T(8,128)} %fusion.35, bf16[512,1024]{0,1:T(8,128)(2,1)S(1)} %get-tuple-element.21, bf16[1024,1024]{1,0:T(8,128)(2,1)S(1)} %copy-done, f32[]{:T(128)S(6)} %div.21, ...), kind=kOutput, calls=%fused_computation.59 | convolution fusion | flops 1076887552 | bytes 11534348 | tf_op jit(solution)/shard_map/dot_general | solution.py:15
  232.7 5.3 %all_to_all.176 = f32[512,2,512]{2,0,1:T(8,128)S(1)} all-to-all(f32[512,2,512]{2,0,1:T(8,128)S(1)} %bitcast.192), channel_id=1, replica_groups={{0,1},{2,3},{4,5},{6,7},{8,9},{10,11},{12,13},{14,15},{16,17},{18,19},{..., dimensions={1} | all-to-all | bytes 4194304 | tf_op jit(solution)/shard_map/all_to_all | solution.py:65
  242.4 5.4 %all_to_all.177 = f32[2,512,512]{1,2,0:T(8,128)S(1)} all-to-all(f32[2,512,512]{1,2,0:T(8,128)S(1)} %bitcast.195), channel_id=1, replica_groups={{0,1},{2,3},{4,5},{6,7},{8,9},{10,11},{12,13},{14,15},{16,17},{18,19},{..., dimensions={0} | all-to-all | bytes 4194304 | tf_op jit(solution)/shard_map/all_to_all | solution.py:60
  252.2 5.4 %all_to_all.178 = f32[512,2,512]{2,0,1:T(8,128)S(1)} all-to-all(f32[512,2,512]{2,0,1:T(8,128)S(1)} %bitcast.193), channel_id=1, replica_groups={{0,1},{2,3},{4,5},{6,7},{8,9},{10,11},{12,13},{14,15},{16,17},{18,19},{..., dimensions={1} | all-to-all | bytes 4194304 | tf_op jit(solution)/shard_map/all_to_all | solution.py:65
  261.4 3.5 fusion.13
  266.9 29.9 %psum.15 = f32[3]{0:T(128)S(1)} all-reduce(f32[3]{0:T(128)S(1)} %pad_maximum_fusion.1), channel_id=1, replica_groups=mesh['blocks'=2,'mode'=16] {'mode'}, use_global_device_ids=true, to_apply=%region_7.8 | all-reduce | flops 3 | bytes 24 | tf_op jit(solution)/shard_map/psum | solution.py:114
  301.3 7.0 %fusion.12 = (f32[1024,512]{0,1:T(8,128)}, f32[1024,512]{0,1:T(8,128)}) fusion(f32[512,1024]{1,0:T(8,128)} %copy-done.8, f32[1024,512]{0,1:T(8,128)} %copy.55, f32[]{:T(128)S(6)} %div.23, f32[]{:T(128)S(6)} %add.116, f32[1024,512]{0,1:T(8,128)} %get-tuple-element.48, f32[1024,512]{0,1:T(8,128)} %get-tuple-element.45), kind=kLoop, calls=%fused_computation.51 | loop fusion | flops 3145728 | bytes 12582920 | tf_op jit(solution)/shard_map/add | solution.py:118
  311.1 9.3 %all-to-all-start.10 = ((f32[16,64,512]{2,1,0:T(8,128)}), f32[16,64,512]{2,1,0:T(8,128)}, u32[]{:S(2)}, u32[]{:S(2)}) async-start(f32[16,64,512]{2,1,0:T(8,128)} %bitcast.187), calls=%async_computation.10 | async-start | bytes 4194304 | tf_op jit(solution)/shard_map/all_to_all | solution.py:57
  323.3 43.6 %all-to-all-done.10 = f32[16,64,512]{2,1,0:T(8,128)} async-done(((f32[16,64,512]{2,1,0:T(8,128)}), f32[16,64,512]{2,1,0:T(8,128)}, u32[]{:S(2)}, u32[]{:S(2)}) %all-to-all-start.10) | async-done | bytes 2097184 | tf_op jit(solution)/shard_map/all_to_all | solution.py:57
  366.9 6.1 %all-to-all-start.11 = ((f32[16,64,512]{2,1,0:T(8,128)}), f32[16,64,512]{2,1,0:T(8,128)}, u32[]{:S(2)}, u32[]{:S(2)}) async-start(f32[16,64,512]{2,1,0:T(8,128)} %bitcast.186), calls=%async_computation.11 | async-start | bytes 4194304 | tf_op jit(solution)/shard_map/all_to_all | solution.py:57
  373.0 4.5 %copy.50 = f32[2,4,64,2,512]{4,3,2,1,0:T(2,128)} copy(f32[2,4,64,2,512]{4,2,3,0,1:T(8,128)} %bitcast.57) | data formatting | bytes 4194304 | tf_op jit(solution)/shard_map/transpose | solution.py:72
  377.6 4.0 reshape.81
  381.6 38.0 %all-to-all-done.11 = f32[16,64,512]{2,1,0:T(8,128)} async-done(((f32[16,64,512]{2,1,0:T(8,128)}), f32[16,64,512]{2,1,0:T(8,128)}, u32[]{:S(2)}, u32[]{:S(2)}) %all-to-all-start.11) | async-done | bytes 2097184 | tf_op jit(solution)/shard_map/all_to_all | solution.py:57
  419.6 4.5 %copy.52 = f32[2,4,64,2,512]{4,3,2,1,0:T(2,128)} copy(f32[2,4,64,2,512]{4,2,3,0,1:T(8,128)} %bitcast.60) | data formatting | bytes 4194304 | tf_op jit(solution)/shard_map/transpose | solution.py:72
  424.1 4.0 reshape.84
  428.1 4.1 sub.55
  (100 shorter events, 72.8 us)
Async XLA Ops:
  7.2 21.1 %copy-start = (bf16[1024,1024]{1,0:T(8,128)(2,1)S(1)}, bf16[1024,1024]{1,0:T(8,128)(2,1)}, u32[]{:S(2)}) copy-start(bf16[1024,1024]{1,0:T(8,128)(2,1)} %param.15) | copy-start | bytes 6291460
  19.9 30.3 %all-to-all-start.4 = ((f32[16,64,256]{2,1,0:T(8,128)}), f32[16,64,256]{2,1,0:T(8,128)S(1)}, u32[]{:S(2)}, u32[]{:S(2)}) async-start(f32[16,64,256]{2,1,0:T(8,128)} %bitcast.198), calls=%async_computation.4 | async-start | bytes 2097152 | tf_op jit(solution)/shard_map/all_to_all | solution.py:57
  50.2 6.1 %copy-start.16 = (f32[8]{0:T(128)S(1)}, f32[8]{0:T(128)}, u32[]{:S(2)}) copy-start(f32[8]{0:T(128)} %param.11) | copy-start | bytes 100
  50.2 7.3 %copy-start.21 = (u32[32]{0:T(128)S(1)}, u32[32]{0:T(128)}, u32[]{:S(2)}) copy-start(u32[32]{0:T(128)} %constant.78) | copy-start | bytes 388
  50.2 8.6 %copy-start.20 = (f32[64]{0:T(128)S(1)}, f32[64]{0:T(128)}, u32[]{:S(2)}) copy-start(f32[64]{0:T(128)} %param.17) | copy-start | bytes 772
  50.2 64.0 %copy-start.17 = (f32[1024]{0:T(1024)S(1)}, f32[1024]{0:T(1024)}, u32[]{:S(2)}) copy-start(f32[1024]{0:T(1024)} %param.16) | copy-start | bytes 12292
  50.2 67.9 %all-to-all-start = ((f32[16,64,512]{2,1,0:T(8,128)}), f32[16,64,512]{2,1,0:T(8,128)}, u32[]{:S(2)}, u32[]{:S(2)}) async-start(f32[16,64,512]{2,1,0:T(8,128)} %bitcast.184), calls=%async_computation | async-start | bytes 4194304 | tf_op jit(solution)/shard_map/all_to_all | solution.py:57
  56.2 106.7 %all-gather.2.cloned.1.call-start = ((), (), s32[]{:S(2)}) async-start(), calls=%async_computation.12 | async-start | bytes 3145728 | tf_op jit(solution)/shard_map/all_gather | solution.py:82
  118.2 2.2 copy-start.3
  120.4 2.2 copy-start.1
  124.8 1.4 copy-start.6
  137.4 1.3 copy-start.14
  148.0 3.7 copy-start.15
  148.0 3.7 copy-start.18
  158.7 1.6 copy-start.11
  162.9 8.3 %copy-start.7 = (f32[512,1024]{1,0:T(8,128)S(1)}, f32[512,1024]{1,0:T(8,128)}, u32[]{:S(2)}) copy-start(f32[512,1024]{1,0:T(8,128)} %copy-done.6) | copy-start | bytes 6291460
  202.3 3.6 copy-start.4
  202.3 3.6 copy-start.9
  213.4 11.0 %all-to-all-start.5 = ((f32[2,512,512]{1,2,0:T(8,128)}), f32[2,512,512]{1,2,0:T(8,128)}, u32[]{:S(2)}, u32[]{:S(2)}) async-start(f32[2,512,512]{1,2,0:T(8,128)} %bitcast.185), calls=%async_computation.5 | async-start | bytes 4194304 | tf_op jit(solution)/shard_map/all_to_all | solution.py:60
  224.4 5.3 %copy-start.2 = (f32[1024,1024]{0,1:T(8,128)S(1)}, f32[1024,1024]{0,1:T(8,128)}, u32[]{:S(2)}) copy-start(f32[1024,1024]{0,1:T(8,128)} %add_divide_fusion) | copy-start | bytes 12582916
  238.0 1.6 copy-start.5
  242.2 18.3 %copy-start.8 = (f32[512,1024]{1,0:T(8,128)}, f32[512,1024]{1,0:T(8,128)S(1)}, u32[]{:S(2)}) copy-start(f32[512,1024]{1,0:T(8,128)S(1)} %convolution_add_fusion.1) | copy-start | bytes 6291460
  247.8 1.6 copy-start.19
  257.6 1.6 copy-start.12
  259.2 1.6 copy-start.10
  259.2 2.2 copy-start.13
  311.1 55.8 %all-to-all-start.10 = ((f32[16,64,512]{2,1,0:T(8,128)}), f32[16,64,512]{2,1,0:T(8,128)}, u32[]{:S(2)}, u32[]{:S(2)}) async-start(f32[16,64,512]{2,1,0:T(8,128)} %bitcast.187), calls=%async_computation.10 | async-start | bytes 4194304 | tf_op jit(solution)/shard_map/all_to_all | solution.py:57
  366.9 52.7 %all-to-all-start.11 = ((f32[16,64,512]{2,1,0:T(8,128)}), f32[16,64,512]{2,1,0:T(8,128)}, u32[]{:S(2)}, u32[]{:S(2)}) async-start(f32[16,64,512]{2,1,0:T(8,128)} %bitcast.186), calls=%async_computation.11 | async-start | bytes 4194304 | tf_op jit(solution)/shard_map/all_to_all | solution.py:57
Sparse Core Ops, SparseCore 0:
  118.3 39.2 all-gather.1

commit v2 on v1

--- a/solution.py
+++ b/solution.py
@@ -1,6 +1,8 @@
 import jax
 import jax.numpy as jnp
 from jax import lax
+from jax.experimental import pallas as pl
+from jax.experimental.pallas import tpu as pltpu
 from jax.sharding import PartitionSpec as P
 
 ITERS = 2
@@ -27,7 +29,7 @@
     return dot(high, matrix, dims) + dot(low, matrix, dims)
 
 
-def body(
+def general_body(
     right_side,
     classes,
     noise_table,
@@ -120,6 +122,464 @@
     return solution_field, right_side - applied
 
 
+LANES = 128
+CHUNK = 128
+TILE = 256
+F32 = jnp.float32
+BF16 = jnp.bfloat16
+
+
+def chip_kernel(
+    dims, table, right, classes, tile_two, eig_one, kern_one, kern_two, base_one, base_two,
+    sol_out, res_out,
+    turned, incoming, level, noise, eig_tiles, eig_row, base_one_t, base_two_t,
+    high, low, right_high, right_low, spectrum, spec_rows, dir_rows, dir_cols, image,
+    later, work, send, recv, sums, totals, applied_in,
+    big_send, big_recv, twin_send, twin_recv, ex_send, ex_recv,
+):
+    M, S, PL, rows, width, height = dims
+    HR, HC = height // 2, width // 2
+    part = HC // S
+    per = width // M
+    line = lax.axis_index("blocks")
+    me = lax.axis_index("mode")
+    mine = lax.rem(me, 2)
+    other = 1 - mine
+    field = me // 2
+    my_plane, my_sample = field // S, lax.rem(field, S)
+    barrier = pltpu.get_barrier_semaphore()
+
+    def device(m):
+        return (line, m)
+
+    @pl.loop(1, M)
+    def _(d):
+        pl.semaphore_signal(barrier, inc=1, device_id=device(lax.rem(me + d, M)), device_id_type=pl.DeviceIdType.MESH)
+
+    def remote(src, dst, sem_send, sem_recv, m):
+        return pltpu.make_async_remote_copy(
+            src_ref=src, dst_ref=dst, send_sem=sem_send, recv_sem=sem_recv,
+            device_id=device(m), device_id_type=pl.DeviceIdType.MESH,
+        )
+
+    def place(m):
+        f = m // 2
+        return f // S, lax.rem(f, S), lax.rem(m, 2)
+
+    def rows_of(index, size, count):
+        return pl.ds(pl.multiple_of(index * size, size), count)
+
+    def block(index, size):
+        return rows_of(index, size, size)
+
+    def copy_turned(d):
+        m = lax.rem(me + d, M)
+        p, s, c = place(m)
+        return remote(
+            turned.at[c, block(s * PL + p, rows)], incoming.at[block(me, rows)],
+            big_send.at[0, d], big_recv.at[0, d], m,
+        )
+
+    def copy_level(d):
+        m = lax.rem(me + d, M)
+        p, s, c = place(m)
+        return remote(
+            level.at[p, :, block(c * S + s, part)], noise.at[s, block(me, rows)],
+            big_send.at[1, d], big_recv.at[1, d], m,
+        )
+
+    def copy_eig(d):
+        m = lax.rem(me + d, M)
+        return remote(eig_tiles.at[me], eig_tiles.at[me], big_send.at[2, d], big_recv.at[2, d], m)
+
+    def copy_total(which, d):
+        m = lax.rem(me + d, M)
+        return remote(
+            totals.at[which, me], totals.at[which, me],
+            big_send.at[3 + which, d], big_recv.at[3 + which, d], m,
+        )
+
+    def copy_sol(d):
+        m = lax.rem(me + d, M)
+        return remote(
+            dir_cols.at[block(m, rows)], sol_out.at[my_sample, my_plane, :, block(mine, HC)],
+            big_send.at[5, d], big_recv.at[5, d], m,
+        )
+
+    def copy_applied(d):
+        m = lax.rem(me + d, M)
+        return remote(
+            image.at[block(m, rows)], applied_in.at[me],
+            big_send.at[6, d], big_recv.at[6, d], m,
+        )
+
+    def copy_twin(o):
+        s = lax.rem(my_sample + o, S)
+        return remote(
+            noise.at[my_sample], noise.at[my_sample], twin_send.at[o], twin_recv.at[o],
+            (my_plane * S + s) * 2 + mine,
+        )
+
+    def copy_near(e, src):
+        return remote(src, recv.at[e], ex_send.at[e], ex_recv.at[e], me - mine + other)
+
+    def split_to(hi, lo, value, *index):
+        h = value.astype(BF16)
+        hi[index] = h
+        lo[index] = (value - h.astype(F32)).astype(BF16)
+
+    def mxu(a, b):
+        return jnp.dot(a, b, preferred_element_type=F32)
+
+    def chunks(fn):
+        @pl.loop(0, HR // CHUNK)
+        def _(i):
+            fn(pl.multiple_of(i * CHUNK, CHUNK))
+
+    def split_half(k, get):
+        def one(i):
+            split_to(high, low, get(i), k, pl.ds(i, CHUNK), slice(None))
+
+        chunks(one)
+
+    def product(left, mat, h, ks, out, add=False):
+        @pl.loop(0, HC // TILE)
+        def _(n):
+            lane = pl.multiple_of(n * TILE, TILE)
+            total = None
+            for k in ks:
+                if left:
+                    a = mat[block(h, HR), block(k, HR)]
+                    term = mxu(a, high[k, :, pl.ds(lane, TILE)]) + mxu(a, low[k, :, pl.ds(lane, TILE)])
+                else:
+                    b = mat[block(k, HC), pl.ds(pl.multiple_of(h * HC + lane, TILE), TILE)]
+                    term = mxu(high[k], b) + mxu(low[k], b)
+                total = term if total is None else total + term
+            if add:
+                total = total + out[:, pl.ds(lane, TILE)]
+            out[:, pl.ds(lane, TILE)] = total
+
+    def arrive(e):
+        copy_near(e, send.at[0]).wait_recv()
+        split_half(other, lambda i: recv[e, pl.ds(i, CHUNK)])
+
+    def both(left, mat, outs, source=None):
+        if source is None:
+            for h, out in outs:
+                product(left, mat, h, (0, 1), out)
+        else:
+            for h, out in outs:
+                product(left, mat, h, (mine,), out)
+            arrive(source)
+            for h, out in outs:
+                product(left, mat, h, (other,), out, True)
+
+    def cross(left, mat, e, slot, own, source=None):
+        out = send.at[slot]
+        if source is None:
+            product(left, mat, other, (0, 1), out)
+            copy_near(e, out).start()
+            product(left, mat, mine, (0, 1), own)
+        else:
+            product(left, mat, other, (mine,), out)
+            product(left, mat, mine, (mine,), own)
+            arrive(source)
+            product(left, mat, other, (other,), out, True)
+            copy_near(e, out).start()
+            product(left, mat, mine, (other,), own, True)
+        split_half(mine, lambda i: own[pl.ds(i, CHUNK)])
+
+    def add_sum(index, value):
+        sums[index] += jnp.sum(value.reshape(CHUNK // 8, 8, HC), axis=0)
+
+    def start_total(which, count):
+        line_index = lax.broadcasted_iota(jnp.int32, (8, LANES), 0)
+        tile = jnp.zeros((8, LANES), F32)
+        for q in range(count):
+            tile = jnp.where(line_index == q, jnp.sum(sums[2 * which + q]), tile)
+        totals[which, me] = tile
+
+        @pl.loop(1, M)
+        def _(d):
+            copy_total(which, d).start()
+
+    def end_total(which):
+        @pl.loop(1, M)
+        def _(d):
+            copy_total(which, d).wait()
+
+        return jnp.sum(totals[which], axis=0)
+
+    sums[...] = jnp.zeros_like(sums)
+    count = S * PL * rows
+
+    @pl.loop(0, S)
+    def _(s):
+        @pl.loop(0, PL)
+        def _(p):
+            split_to(right_high, right_low, right[s, p], block(s * PL + p, rows), slice(None))
+
+    def turn(c):
+        @pl.loop(0, HC // TILE)
+        def _(n):
+            lane = pl.multiple_of(n * TILE, TILE)
+            b = base_two[:, pl.ds(pl.multiple_of(c * HC + lane, TILE), TILE)]
+            turned[c, :, pl.ds(lane, TILE)] = mxu(right_high[...], b) + mxu(right_low[...], b)
+
+    pl.semaphore_wait(barrier, M - 1)
+    eig_tiles[me] = tile_two[...]
+
+    @pl.loop(1, M)
+    def _(d):
+        copy_eig(d).start()
+
+    turn(mine)
+
+    @pl.loop(1, M // 2)
+    def _(i):
+        copy_turned(2 * i).start()
+
+    turn(other)
+
+    @pl.loop(0, M // 2)
+    def _(i):
+        copy_turned(2 * i + 1).start()
+
+    incoming[block(me, rows)] = turned[mine, block(my_sample * PL + my_plane, rows)]
+
+    @pl.loop(0, PL)
+    def _(p):
+        kind = classes[p]
+        value = jnp.full(kind.shape, table[0], F32)
+        for index in range(1, table.shape[0]):
+            value = jnp.where(kind == index, table[index], value)
+        level[p] = value
+
+    @pl.loop(1, M)
+    def _(d):
+        copy_level(d).start()
+
+    noise[my_sample, block(me, rows)] = level[my_plane, :, block(mine * S + my_sample, part)]
+    mean_noise = table[0]
+    for index in range(1, table.shape[0]):
+        mean_noise = mean_noise + table[index]
+    mean_noise = mean_noise / table.shape[0]
+
+    for a in range(height // TILE):
+        for b in range(height // TILE):
+            sa, sb = slice(a * TILE, (a + 1) * TILE), slice(b * TILE, (b + 1) * TILE)
+            base_one_t[sa, sb] = base_one[sb, sa].astype(F32).T.astype(BF16)
+    for a in range(width // TILE):
+        for b in range(width // TILE):
+            sa, sb = slice(a * TILE, (a + 1) * TILE), slice(b * TILE, (b + 1) * TILE)
+            base_two_t[sa, sb] = base_two[sb, sa].astype(F32).T.astype(BF16)
+
+    @pl.loop(1, M)
+    def _(d):
+        copy_eig(d).wait()
+
+    fold = LANES // per
+    for k in range(width // LANES):
+        total = eig_tiles[k * fold]
+        for q in range(1, fold):
+            total = total + eig_tiles[k * fold + q]
+        eig_row[:, k * LANES:(k + 1) * LANES] = total
+
+    def weights(row, half):
+        e2 = eig_row[0:1, block(half, HC)]
+        return 1.0 / (eig_one[pl.ds(row, CHUNK), :] * e2 + mean_noise)
+
+    @pl.loop(1, M)
+    def _(d):
+        copy_turned(d).wait()
+
+    for k in range(2):
+        split_half(k, lambda i: incoming[pl.ds(k * HR + i, CHUNK)])
+    both(True, base_one_t, [(h, spectrum.at[h]) for h in range(2)])
+    copy_near(0, spectrum.at[other]).start()
+    for h in range(2):
+        def weigh(i):
+            value = spectrum[h, pl.ds(i, CHUNK)]
+            scaled = weights(pl.multiple_of(h * HR + i, CHUNK), mine) * value
+            add_sum(0, value * scaled)
+            split_to(high, low, scaled, h, pl.ds(i, CHUNK), slice(None))
+
+        chunks(weigh)
+    cross(True, base_one, 1, 0, work)
+    both(False, base_two_t, [(h, dir_rows.at[h]) for h in range(2)], 1)
+    copy_near(2, dir_rows.at[other]).start()
+    for h in range(2):
+        split_half(h, lambda i: dir_rows[h, pl.ds(i, CHUNK)])
+    cross(False, kern_two, 3, 1, work)
+
+    both(True, kern_one, [(h, image.at[pl.ds(h * HR, HR)]) for h in range(2)], 3)
+
+    @pl.loop(1, M)
+    def _(d):
+        copy_level(d).wait()
+
+    for o in range(1, S):
+        copy_twin(o).start()
+    copy_near(2, dir_rows.at[other]).wait_recv()
+    dir_cols[block(mine, HR)] = dir_rows[mine]
+    dir_cols[block(other, HR)] = recv[2]
+    for o in range(1, S):
+        copy_twin(o).wait()
+
+    def noisy(row, value):
+        local = jnp.concatenate([noise[s, pl.ds(row, CHUNK)] for s in range(S)], axis=1)
+        return local * value
+
+    for h in range(2):
+        def finish(i):
+            row = pl.multiple_of(h * HR + i, CHUNK)
+            value = dir_cols[pl.ds(row, CHUNK)]
+            result = image[pl.ds(row, CHUNK)] + noisy(row, value)
+            image[pl.ds(row, CHUNK)] = result
+            add_sum(1, value * result)
+            split_to(high, low, result, h, pl.ds(i, CHUNK), slice(None))
+
+        chunks(finish)
+    start_total(0, 2)
+    cross(True, base_one_t, 4, 2, work)
+    both(False, base_two, [(h, spec_rows.at[h]) for h in range(2)], 4)
+    copy_near(0, spectrum.at[other]).wait_recv()
+    first = end_total(0)
+    gamma, curvature = first[0:1, 0:1], first[1:2, 0:1]
+    alpha = gamma / curvature
+
+    def next_weigh(h, get):
+        def one(i):
+            value = get(i) - alpha * spec_rows[h, pl.ds(i, CHUNK)]
+            scaled = weights(pl.multiple_of(mine * HR + i, CHUNK), h) * value
+            add_sum(2, value * scaled)
+            split_to(high, low, scaled, h, pl.ds(i, CHUNK), slice(None))
+
+        chunks(one)
+
+    next_weigh(mine, lambda i: spectrum[mine, pl.ds(i, CHUNK)])
+    next_weigh(other, lambda i: recv[0, pl.ds(i, CHUNK)])
+    cross(False, base_two_t, 5, 3, work)
+    both(True, base_one, [(h, later.at[pl.ds(h * HR, HR)]) for h in range(2)], 5)
+    copy_near(6, later.at[block(other, HR)]).start()
+    split_half(mine, lambda i: later[pl.ds(pl.multiple_of(mine * HR + i, CHUNK), CHUNK)])
+    cross(False, kern_two, 7, 4, work, 6)
+    both(True, kern_one, [(h, spec_rows.at[h]) for h in range(2)], 7)
+    for h in range(2):
+        def finish_later(i):
+            row = pl.multiple_of(h * HR + i, CHUNK)
+            value = later[pl.ds(row, CHUNK)]
+            result = spec_rows[h, pl.ds(i, CHUNK)] + noisy(row, value)
+            spec_rows[h, pl.ds(i, CHUNK)] = result
+            add_sum(3, value * result)
+            add_sum(4, value * image[pl.ds(row, CHUNK)])
+
+        chunks(finish_later)
+    start_total(1, 3)
+    for e, ref in ((0, spectrum.at[other]), (1, send.at[0]), (2, dir_rows.at[other]), (3, send.at[1]),
+                   (4, send.at[2]), (5, send.at[3]), (6, later.at[block(other, HR)]), (7, send.at[4])):
+        copy_near(e, ref).wait_send()
+    second_total = end_total(1)
+    gamma_new, own, mixed = second_total[0:1, 0:1], second_total[1:2, 0:1], second_total[2:3, 0:1]
+    ratio = gamma_new / gamma
+    step = gamma_new / (own + ratio * (2.0 * mixed + ratio * curvature))
+    before = alpha + step * ratio
+
+    def combine(m):
+        spot = block(m, rows)
+        half, inner = m // (M // 2), block(lax.rem(m, M // 2), rows)
+        dir_cols[spot] = before * dir_cols[spot] + step * later[spot]
+        image[spot] = before * image[spot] + step * spec_rows[half, inner]
+
+    @pl.loop(1, M)
+    def _(d):
+        combine(lax.rem(me + d, M))
+        copy_applied(d).start()
+        copy_sol(d).start()
+
+    combine(me)
+    sol_out[my_sample, my_plane, :, block(mine, HC)] = dir_cols[block(me, rows)]
+    res_out[my_sample, my_plane, :, block(mine, HC)] = (
+        right[my_sample, my_plane, :, block(mine, HC)] - image[block(me, rows)]
+    )
+
+    @pl.loop(1, M)
+    def _(d):
+        copy_applied(d).wait()
+        source = lax.rem(me + M - d, M)
+        p, s, c = place(source)
+        spot = block(c, HC)
+        res_out[s, p, :, spot] = right[s, p, :, spot] - applied_in[source]
+
+    @pl.loop(1, M)
+    def _(d):
+        copy_sol(d).wait()
+
+
+def chip_body(
+    right_side, classes, noise_table, kernel_first, kernel_second, basis_first, basis_second,
+    eigen_first, eigen_second,
+):
+    M = lax.axis_size("mode")
+    S, PL, rows, width = right_side.shape
+    height = eigen_first.shape[0]
+    HR, HC = height // 2, width // 2
+    per = eigen_second.shape[0]
+    fold = LANES // per
+    spot = lax.rem(lax.axis_index("mode"), fold)
+    lanes = jnp.arange(LANES)
+    tile = jnp.where(lanes // per == spot, jnp.tile(eigen_second, fold), 0.0)
+    tile = jnp.broadcast_to(tile[None], (8, LANES))
+    vmem = pl.BlockSpec(memory_space=pltpu.VMEM)
+    smem = pl.BlockSpec(memory_space=pltpu.SMEM)
+    V = pltpu.VMEM
+    field = jax.ShapeDtypeStruct(right_side.shape, F32)
+    halves = V((2, HR, HC), F32)
+    whole = V((height, HC), F32)
+
+    def kernel(*refs):
+        chip_kernel((M, S, PL, rows, width, height), *refs)
+
+    return pl.pallas_call(
+        kernel,
+        out_shape=(field, field),
+        in_specs=[smem] + [vmem] * 8,
+        out_specs=(vmem, vmem),
+        scratch_shapes=[
+            V((2, S * PL * rows, HC), F32), whole, V((PL, rows, width), F32),
+            V((S, height, HC // S), F32), V((M, 8, LANES), F32), V((8, width), F32),
+            V((height, height), BF16), V((width, width), BF16),
+            V((2, HR, HC), BF16), V((2, HR, HC), BF16),
+            V((S * PL * rows, width), BF16), V((S * PL * rows, width), BF16),
+            halves, halves, halves, whole, whole, whole, V((HR, HC), F32),
+            V((5, HR, HC), F32), V((8, HR, HC), F32), V((5, 8, HC), F32),
+            V((2, M, 8, LANES), F32), V((M, rows, HC), F32),
+            pltpu.SemaphoreType.DMA((7, M)), pltpu.SemaphoreType.DMA((7, M)),
+            pltpu.SemaphoreType.DMA((S,)), pltpu.SemaphoreType.DMA((S,)),
+            pltpu.SemaphoreType.DMA((8,)), pltpu.SemaphoreType.DMA((8,)),
+        ],
+        compiler_params=pltpu.CompilerParams(
+            collective_id=0, has_side_effects=True, vmem_limit_bytes=60 * 2**20
+        ),
+    )(noise_table, right_side, classes, tile, eigen_first.reshape(height, 1),
+      kernel_first, kernel_second, basis_first, basis_second)
+
+
+def body(right_side, classes, noise_table, kernel_first, kernel_second, basis_first, basis_second,
+         eigen_first, eigen_second):
+    args = (right_side, classes, noise_table, kernel_first, kernel_second, basis_first, basis_second,
+            eigen_first, eigen_second)
+    M = lax.axis_size("mode")
+    S, PL, rows, width = right_side.shape
+    height = eigen_first.shape[0]
+    fits = (
+        M == 2 * S * PL and rows % 16 == 0 and height % (2 * TILE) == 0
+        and width % (2 * max(TILE, LANES * S)) == 0 and LANES % eigen_second.shape[0] == 0
+        and max(height, width) <= 1024
+    )
+    return chip_body(*args) if fits else general_body(*args)
+
+
 def solution(mesh):
     in_specs = (
         P(None, "blocks", "mode", None),

time: 447 us -> 244 us (0.55); the launches traced: 440 us -> 244 us
  Pallas kernels: 0 us -> 236 us
  blocking collectives: 155 us -> 0 us
  waiting for transfers between devices: 92.5 us -> 0 us
  matrix products: 52.8 us -> 0 us
  local copies, waits for them, and re-layouts: 53.4 us -> 7.67 us
  starting transfers between devices: 33 us -> 0 us
  other arithmetic: 32 us -> 0.01 us
  between operations: 21.2 us -> 0.65 us
    pallas_call x0 -> x1, Pallas kernels: none -> 236 us  [chip_body(): pl.pallas_call(kernel, out_shape=(field, field), in_specs=[smem] + [vmem]...]
    all_to_all x5 -> x0, waiting for transfers between devices: 92.4 us -> none  [the longest x4 92.4 us: to_all(): lax.all_to_all(blocks, 'mode', split_axis=0, concat_axis=0, tiled=True)]
    psum x2 -> x0, blocking collectives: 58.9 us -> none  [the longest x1 29.9 us: body(): gamma_new, own, cross = lax.psum(parts, 'mode')]
    unnamed x1 -> x0, blocking collectives: 55.2 us -> none
    dot_general x24 -> x0, matrix products: 52.8 us -> none  [dot(): lax.dot_general(left, right, (dims, ((), ())), preferred_element_type=jnp...]
    all_to_all x7 -> x0, blocking collectives: 40.7 us -> none  [the longest x4 22.6 us: to_columns(): lax.all_to_all(field, 'mode', split_axis=1, concat_axis=0, axis_index_gro...]
    all_to_all x5 -> x0, starting transfers between devices: 33 us -> none  [the longest x4 27.7 us: to_all(): lax.all_to_all(blocks, 'mode', split_axis=0, concat_axis=0, tiled=True)]
    reshape x7 -> x1, local copies, waits for them, and re-layouts: 20.9 us -> 1.71 us  [chip_body(): eigen_first.reshape(height, 1)]
  transfers between devices with their start and end apart: 6 -> 0, of which waited for: 3 -> 0; matrix products, arithmetic and copies ran while one was open for 13% -> 0% of each run, Pallas kernels for 0% -> 0%
where the time goes in v2:
time: 244 us
  Pallas kernels  236 us (97%)
  local copies, waits for them, and re-layouts  7.67 us (3%)
    pallas_call x1, Pallas kernels, chip_body(): pl.pallas_call(kernel, out_shape=(field, field), in_specs=[smem] + [vmem]...  236 us

profile of v2, /device:TPU:29, one launch (start us, length us, event | category | flops | bytes accessed | tf_op | source)
XLA Modules:
  0.0 244.2 jit_solution(4322763584523695796)
XLA Ops:
  0.6 0.7 tile.4
  1.3 0.1 tile.10
  1.4 0.6 broadcast_in_dim.11.refs_3_
  2.0 1.7 copy.11.refs_4_
  3.7 235.8 %shard_map.104 = (f32[2,4,64,1024]{3,2,1,0:T(8,128)}, f32[2,4,64,1024]{3,2,1,0:T(8,128)}) custom-call(f32[8]{0:T(128)} %refs_0_.1, f32[2,4,64,1024]{3,2,1,0:T(8,128)} %refs_1_.1, s32[4,64,1024]{2,1,0:T(8,128)} %refs_2_.1, f32[8,128]{1,0:T(8,128)} %broadcast_in_dim.11.refs_3_, f32[1024,1]{1,0:T(8,128)} %copy.11.refs_4_, bf16[1024,1024]{1,0:T(8,128)(2,1)} %refs_5_.1, ...), custom_call_target="tpu_custom_call" | custom-call | tf_op jit(solution)/shard_map/pallas_call | solution.py:543
  239.5 0.0 copy-start
  239.6 3.3 %copy.14 = f32[2,4,64,1024]{3,2,1,0:T(8,128)} copy(f32[2,4,64,1024]{3,2,1,0:T(8,128)} %get-tuple-element.4) | data formatting | bytes 4194304
  242.9 0.0 copy-done
  242.9 1.3 copy.15
  (1 shorter events, 0.0 us)
Async XLA Ops:
  239.5 3.3 %copy-start = (f32[2,4,64,1024]{3,2,1,0:T(8,128)S(1)}, f32[2,4,64,1024]{3,2,1,0:T(8,128)}, u32[]{:S(2)}) copy-start(f32[2,4,64,1024]{3,2,1,0:T(8,128)} %get-tuple-element.5) | copy-start | bytes 6291460

commit v3 on v2

--- a/solution.py
+++ b/solution.py
@@ -213,12 +213,19 @@
             big_send.at[6, d], big_recv.at[6, d], m,
         )
 
-    def copy_twin(o):
+    def copy_twin(o, d):
         s = lax.rem(my_sample + o, S)
+        spot = noise.at[my_sample, block(lax.rem(me + M - d, M), rows)]
         return remote(
-            noise.at[my_sample], noise.at[my_sample], twin_send.at[o], twin_recv.at[o],
-            (my_plane * S + s) * 2 + mine,
-        )
+            spot, spot, twin_send.at[o, d], twin_recv.at[o, d], (my_plane * S + s) * 2 + mine
+        )
+
+    def forward(first, end):
+        @pl.loop(first, end)
+        def _(d):
+            copy_level(d).wait_recv()
+            for o in range(1, S):
+                copy_twin(o, d).start()
 
     def copy_near(e, src):
         return remote(src, recv.at[e], ex_send.at[e], ex_recv.at[e], me - mine + other)
@@ -360,6 +367,8 @@
         copy_level(d).start()
 
     noise[my_sample, block(me, rows)] = level[my_plane, :, block(mine * S + my_sample, part)]
+    for o in range(1, S):
+        copy_twin(o, 0).start()
     mean_noise = table[0]
     for index in range(1, table.shape[0]):
         mean_noise = mean_noise + table[index]
@@ -405,26 +414,30 @@
             split_to(high, low, scaled, h, pl.ds(i, CHUNK), slice(None))
 
         chunks(weigh)
+    forward(1, 1 + M // 3)
     cross(True, base_one, 1, 0, work)
     both(False, base_two_t, [(h, dir_rows.at[h]) for h in range(2)], 1)
     copy_near(2, dir_rows.at[other]).start()
     for h in range(2):
         split_half(h, lambda i: dir_rows[h, pl.ds(i, CHUNK)])
+    forward(1 + M // 3, 1 + 2 * (M // 3))
     cross(False, kern_two, 3, 1, work)
 
     both(True, kern_one, [(h, image.at[pl.ds(h * HR, HR)]) for h in range(2)], 3)
 
-    @pl.loop(1, M)
-    def _(d):
-        copy_level(d).wait()
-
-    for o in range(1, S):
-        copy_twin(o).start()
+    forward(1 + 2 * (M // 3), M)
     copy_near(2, dir_rows.at[other]).wait_recv()
     dir_cols[block(mine, HR)] = dir_rows[mine]
     dir_cols[block(other, HR)] = recv[2]
-    for o in range(1, S):
-        copy_twin(o).wait()
+
+    @pl.loop(0, M)
+    def _(d):
+        for o in range(1, S):
+            copy_twin(o, d).wait()
+
+    @pl.loop(1, M)
+    def _(d):
+        copy_level(d).wait_send()
 
     def noisy(row, value):
         local = jnp.concatenate([noise[s, pl.ds(row, CHUNK)] for s in range(S)], axis=1)
@@ -555,7 +568,7 @@
             V((5, HR, HC), F32), V((8, HR, HC), F32), V((5, 8, HC), F32),
             V((2, M, 8, LANES), F32), V((M, rows, HC), F32),
             pltpu.SemaphoreType.DMA((7, M)), pltpu.SemaphoreType.DMA((7, M)),
-            pltpu.SemaphoreType.DMA((S,)), pltpu.SemaphoreType.DMA((S,)),
+            pltpu.SemaphoreType.DMA((S, M)), pltpu.SemaphoreType.DMA((S, M)),
             pltpu.SemaphoreType.DMA((8,)), pltpu.SemaphoreType.DMA((8,)),
         ],
         compiler_params=pltpu.CompilerParams(

time: 244 us -> 231 us (0.947)
  Pallas kernels: 236 us -> 223 us
    pallas_call x1, Pallas kernels: 236 us -> 223 us  [chip_body(): pl.pallas_call(kernel, out_shape=(field, field), in_specs=[smem] + [vmem]...]
where the time goes in v3:
time: 231 us
  Pallas kernels  223 us (97%)
  local copies, waits for them, and re-layouts  7.67 us (3%)
    pallas_call x1, Pallas kernels, chip_body(): pl.pallas_call(kernel, out_shape=(field, field), in_specs=[smem] + [vmem]...  223 us
    unnamed x4, local copies, waits for them, and re-layouts  4.63 us

profile of v3, /device:TPU:29, one launch (start us, length us, event | category | flops | bytes accessed | tf_op | source)
XLA Modules:
  0.0 231.2 jit_solution(6680063405985073226)
XLA Ops:
  0.6 0.7 tile.4
  1.3 0.1 tile.10
  1.4 0.6 broadcast_in_dim.11.refs_3_
  2.0 1.7 copy.11.refs_4_
  3.7 222.8 %shard_map.104 = (f32[2,4,64,1024]{3,2,1,0:T(8,128)}, f32[2,4,64,1024]{3,2,1,0:T(8,128)}) custom-call(f32[8]{0:T(128)} %refs_0_.1, f32[2,4,64,1024]{3,2,1,0:T(8,128)} %refs_1_.1, s32[4,64,1024]{2,1,0:T(8,128)} %refs_2_.1, f32[8,128]{1,0:T(8,128)} %broadcast_in_dim.11.refs_3_, f32[1024,1]{1,0:T(8,128)} %copy.11.refs_4_, bf16[1024,1024]{1,0:T(8,128)(2,1)} %refs_5_.1, ...), custom_call_target="tpu_custom_call" | custom-call | tf_op jit(solution)/shard_map/pallas_call | solution.py:556
  226.5 0.0 copy-start
  226.5 3.3 %copy.14 = f32[2,4,64,1024]{3,2,1,0:T(8,128)} copy(f32[2,4,64,1024]{3,2,1,0:T(8,128)} %get-tuple-element.4) | data formatting | bytes 4194304
  229.8 0.0 copy-done
  229.8 1.3 copy.15
  (1 shorter events, 0.0 us)
Async XLA Ops:
  226.5 3.3 %copy-start = (f32[2,4,64,1024]{3,2,1,0:T(8,128)S(1)}, f32[2,4,64,1024]{3,2,1,0:T(8,128)}, u32[]{:S(2)}) copy-start(f32[2,4,64,1024]{3,2,1,0:T(8,128)} %get-tuple-element.5) | copy-start | bytes 6291460
